TPU v7x, 512 devices: a whole 4x8x8 slice. The times are simulated.
512 devices in a mesh: replica: 8 (over y_hi, core), fsdp: 8 (over x, y_lo), tensor: 8 (over z).
Axes of the slice: x: 4, y: 8 (y_hi: 4, y_lo: 2; y = y_hi * 2 + y_lo), z: 8, core: 2. Of those that a mesh axis runs over, the one named last changes fastest.
Arguments:
- grad_parts: bfloat16 [8, 8, 512, 8192], P('replica', 'fsdp', 'tensor'), may hold values from -12 to 12
- inner_params: float32 [8, 512, 8192], P('replica', 'tensor', 'fsdp'), may hold values from -0.12 to 0.12
- first_moment: float32 [8, 512, 8192], P('replica', 'tensor', 'fsdp'), may hold values from -4 to 4
- second_moment: float32 [8, 512, 8192], P('replica', 'tensor', 'fsdp'), may hold values from 0.1 to 10
- outer_params: float32 [8, 512, 1024], P('replica', 'tensor', 'fsdp'), may hold values from -0.12 to 0.12
- outer_momentum: float32 [8, 512, 1024], P('replica', 'tensor', 'fsdp'), may hold values from -0.06 to 0.06
Outputs:
- next_weights: float32 [512, 8192], P('tensor')
- outer_params_out: float32 [8, 512, 1024], P('replica', 'tensor', 'fsdp')
- outer_momentum_out: float32 [8, 512, 1024], P('replica', 'tensor', 'fsdp')
- first_out: float32 [8, 512, 8192], P('replica', 'tensor', 'fsdp')
- second_out: float32 [8, 512, 8192], P('replica', 'tensor', 'fsdp')
All inputs are finite; a program needn't handle non-finite values.
Results may differ from a plain program's by a relative error of at most 0.0003.
Values may be sent and summed in bfloat16 or wider, within the bound.
A program may use at most 64 MiB of HBM per device.

v0:
```python
import jax
import jax.numpy as jnp
from jax import lax
from jax.sharding import PartitionSpec as P

STEP = 100


beta_first = 0.9
beta_second = 0.95
inner_rate = 0.01
weight_decay = 0.1
epsilon = 1e-08
outer_rate = 0.7
momentum_factor = 0.9


def inner_adamw(gradient, params, first_in, second_in):
    first_out = beta_first * first_in + (1.0 - beta_first) * gradient
    second_out = beta_second * second_in + (1.0 - beta_second) * gradient * gradient
    first_scale = 1.0 / (1.0 - beta_first**STEP)
    second_scale = 1.0 / (1.0 - beta_second**STEP)
    direction = first_out * first_scale / (jnp.sqrt(second_out * second_scale) + epsilon)
    updated = params - inner_rate * (direction + weight_decay * params)
    return (first_out, second_out, updated)


def nesterov(mean_params, outer_in, momentum):
    pseudo_grad = outer_in - mean_params
    momentum_new = momentum_factor * momentum + pseudo_grad
    params_new = outer_in - outer_rate * (pseudo_grad + momentum_factor * momentum_new)
    return (params_new, momentum_new)


def local(grad_parts, inner_params, first_moment, second_moment, outer_params, outer_momentum):
    replicas = lax.axis_size("replica")
    gradient = lax.psum_scatter(
        grad_parts[0, 0].astype(jnp.float32), "fsdp", scatter_dimension=1, tiled=True
    )
    first_out, second_out, updated = inner_adamw(
        gradient, inner_params[0], first_moment[0], second_moment[0]
    )
    share_cols = outer_params.shape[2]
    totals = lax.psum_scatter(updated, "replica", scatter_dimension=1, tiled=True)
    params_new, momentum_new = nesterov(totals / replicas, outer_params[0], outer_momentum[0])
    pieces = lax.all_gather(params_new[None], ("replica", "fsdp"), axis=0, tiled=True)
    fsdp_count = lax.axis_size("fsdp")
    row_count = params_new.shape[0]
    arranged = pieces.reshape(replicas, fsdp_count, row_count, share_cols).transpose(2, 1, 0, 3)
    next_weights = arranged.reshape(row_count, fsdp_count * replicas * share_cols)
    return (next_weights, params_new[None], momentum_new[None], first_out[None], second_out[None])


def solution(mesh):
    return jax.shard_map(
        local,
        mesh=mesh,
        in_specs=(
            P("replica", "fsdp", "tensor", None),
            P("replica", "tensor", "fsdp"),
            P("replica", "tensor", "fsdp"),
            P("replica", "tensor", "fsdp"),
            P("replica", "tensor", "fsdp"),
            P("replica", "tensor", "fsdp"),
        ),
        out_specs=(
            P("tensor", None),
            P("replica", "tensor", "fsdp"),
            P("replica", "tensor", "fsdp"),
            P("replica", "tensor", "fsdp"),
            P("replica", "tensor", "fsdp"),
        ),
        check_vma=False,
    )
```

profile of v0, /device:TPU:1, one launch (start us, length us, event | category | flops | bytes accessed | tf_op | source)
XLA Modules:
  0.0 314.8 jit_solution(140816318661857395)
XLA Ops:
  7.2 0.0 copy-start
  7.2 0.0 copy-start.1
  7.2 0.0 copy-start.2
  7.2 0.0 reduce-scatter.3.cloned.1.call-start
  7.2 2.7 bitcast_convert_fusion
  10.0 0.0 copy-start.3
  10.0 0.0 copy-start.4
  10.0 0.0 reduce-scatter.3.cloned.1.call-update
  10.0 0.0 reduce-scatter.5.cloned.1.call-start
  10.1 64.5 %reduce-scatter.3.cloned.1.call-done = f32[64,1024]{1,0:T(8,128)} async-done(((f32[64,8192]{1,0:T(8,128)}), f32[64,1024]{1,0:T(8,128)}) %reduce-scatter.3.cloned.1.call-update) | async-done | bytes 262160 | tf_op jit(solution)/shard_map/reduce_scatter | solution.py:37
  74.6 0.0 copy-done
  74.6 0.0 copy-done.1
  74.6 0.0 copy-done.2
  74.6 2.0 fusion.4
  76.6 0.0 reduce-scatter.5.cloned.1.call-update
  76.6 0.0 all-gather.3.cloned.1.call-start
  76.7 38.7 %reduce-scatter.5.cloned.1.call-done = f32[64,128]{1,0:T(8,128)} async-done(((f32[64,1024]{1,0:T(8,128)}), f32[64,128]{1,0:T(8,128)}) %reduce-scatter.5.cloned.1.call-update) | async-done | bytes 32784 | tf_op jit(solution)/shard_map/reduce_scatter | solution.py:44
  115.4 0.0 copy-done.3
  115.4 0.0 copy-done.4
  115.4 1.4 fusion.5
  116.8 0.0 all-gather.3.cloned.1.call-update
  116.8 186.2 %all-gather.3.cloned.1.call-done = f32[4096,128]{1,0:T(8,128)} async-done(((f32[64,128]{1,0:T(8,128)}), f32[4096,128]{1,0:T(8,128)}) %all-gather.3.cloned.1.call-update) | async-done | bytes 2097168 | tf_op jit(solution)/shard_map/all_gather | solution.py:46
  303.0 2.8 copy.11
  305.8 2.5 copy.14
Async XLA Ops:
  7.2 67.4 %copy-start = (f32[1,64,1024]{2,1,0:T(8,128)S(1)}, f32[1,64,1024]{2,1,0:T(8,128)}, u32[]{:S(2)}) copy-start(f32[1,64,1024]{2,1,0:T(8,128)} %param.9) | copy-start | bytes 786436
  7.2 67.4 %copy-start.1 = (f32[1,64,1024]{2,1,0:T(8,128)S(1)}, f32[1,64,1024]{2,1,0:T(8,128)}, u32[]{:S(2)}) copy-start(f32[1,64,1024]{2,1,0:T(8,128)} %param.8) | copy-start | bytes 786436
  7.2 67.4 %copy-start.2 = (f32[1,64,1024]{2,1,0:T(8,128)S(1)}, f32[1,64,1024]{2,1,0:T(8,128)}, u32[]{:S(2)}) copy-start(f32[1,64,1024]{2,1,0:T(8,128)} %param.7) | copy-start | bytes 786436
  7.2 67.4 %reduce-scatter.3.cloned.1.call-start = ((), (), s32[]{:S(2)}) async-start(), calls=%async_computation.2 | async-start | bytes 2359296 | tf_op jit(solution)/shard_map/reduce_scatter | solution.py:37
  10.0 105.4 %copy-start.3 = (f32[1,64,128]{2,1,0:T(8,128)S(1)}, f32[1,64,128]{2,1,0:T(8,128)}, u32[]{:S(2)}) copy-start(f32[1,64,128]{2,1,0:T(8,128)} %param.10) | copy-start | bytes 98308
  10.0 105.4 %copy-start.4 = (f32[1,64,128]{2,1,0:T(8,128)S(1)}, f32[1,64,128]{2,1,0:T(8,128)}, u32[]{:S(2)}) copy-start(f32[1,64,128]{2,1,0:T(8,128)} %param.11) | copy-start | bytes 98308
  10.0 105.4 %reduce-scatter.5.cloned.1.call-start = ((), (), s32[]{:S(2)}) async-start(), calls=%async_computation.3 | async-start | bytes 294912 | tf_op jit(solution)/shard_map/reduce_scatter | solution.py:44
  76.6 226.4 %all-gather.3.cloned.1.call-start = ((), (), s32[]{:S(2)}) async-start(), calls=%async_computation.4 | async-start | bytes 2129920 | tf_op jit(solution)/shard_map/all_gather | solution.py:46
Sparse Core Ops, SparseCore 0:
  11.4 63.0 reduce-scatter.2
  77.9 37.4 reduce-scatter.4
  118.3 184.6 all-gather.2
where the time goes:
time: 321 us; the launch traced here: 315 us
  waiting for transfers between devices  289 us (90%)
  between operations  13.8 us (4%)
  other arithmetic  6.15 us (2%)
  local copies, waits for them, and re-layouts  5.34 us (2%)
    all_gather x1, waiting for transfers between devices, local(): lax.all_gather(params_new[None], ('replica', 'fsdp'), axis=0, tiled=True)  186 us
    reduce_scatter x1, waiting for transfers between devices, local(): lax.psum_scatter(grad_parts[0, 0].astype(jnp.float32), 'fsdp', scatter_di...  64.5 us
    reduce_scatter x1, waiting for transfers between devices, local(): lax.psum_scatter(updated, 'replica', scatter_dimension=1, tiled=True)  38.7 us
  transfers between devices with their start and end apart: 3, of which 3 were waited for; matrix products, arithmetic and copies ran while one was open for 0% of the time, Pallas kernels for 0%

commit v1 on v0

--- a/solution.py
+++ b/solution.py
@@ -1,10 +1,13 @@
 import jax
 import jax.numpy as jnp
 from jax import lax
+from jax.experimental import pallas as pl
+from jax.experimental.pallas import tpu as pltpu
 from jax.sharding import PartitionSpec as P
 
+MESH = pl.DeviceIdType.MESH
 STEP = 100
-
+CHUNKS = 4
 
 beta_first = 0.9
 beta_second = 0.95
@@ -13,6 +16,11 @@
 epsilon = 1e-08
 outer_rate = 0.7
 momentum_factor = 0.9
+
+FSDP = [(2, 0), (2, 1), (1, 0), (3, 0), (1, 1), (3, 1), (0, 1)]
+COLUMN = [(2, 0), (2, 1), (1, 0), (3, 0), (1, 1), (3, 1), (0, 1)]
+HIGH = [2, 1, 3]
+ACROSS = [2, 1, 3]
 
 
 def inner_adamw(gradient, params, first_in, second_in):
@@ -32,23 +40,251 @@
     return (params_new, momentum_new)
 
 
+def kernel(
+    g_hbm, p_hbm, m1_hbm, m2_hbm, op_hbm, om_hbm,
+    full, p_out, m_out, first_out, second_out,
+    own, parts, params, first_in, second_in, outer_in, momentum_in,
+    updated, other, pair, sums,
+    local_sem, grad_send, grad_recv, core_send, core_recv, high_send, high_recv,
+    col_send, col_recv, row_send, row_recv, twin_send, twin_recv,
+):
+    replica, f = lax.axis_index("replica"), lax.axis_index("fsdp")
+    yh, core = replica // 2, lax.rem(replica, 2)
+    x, yl = f // 2, lax.rem(f, 2)
+    rows = 64 // CHUNKS
+    tiles = rows // 8
+
+    def at_x(step):
+        return lax.rem(x + step + 4, 4)
+
+    def at_yh(step):
+        return lax.rem(yh + step + 4, 4)
+
+    def at_yl(flip):
+        return 1 - yl if flip else yl
+
+    twin = {"replica": yh * 2 + 1 - core}
+
+    barrier = pltpu.get_barrier_semaphore()
+    peers = [{"fsdp": at_x(s) * 2 + at_yl(flip)} for s, flip in FSDP]
+    peers += [{"replica": at_yh(s) * 2 + core, "fsdp": x * 2 + at_yl(flip)} for s, flip in COLUMN if s]
+    peers += [twin]
+    for peer in peers:
+        pl.semaphore_signal(barrier, inc=1, device_id=peer, device_id_type=MESH)
+
+    mine = pl.ds(pl.multiple_of(f * 1024, 1024), 1024)
+    loads = [
+        pltpu.make_async_copy(src, dst, local_sem.at[i])
+        for i, (src, dst) in enumerate(
+            (
+                (g_hbm.at[:, mine], own),
+                (p_hbm, params),
+                (m1_hbm, first_in),
+                (m2_hbm, second_in),
+                (op_hbm, outer_in),
+                (om_hbm, momentum_in),
+            )
+        )
+    ]
+    for load in loads:
+        load.start()
+    pl.semaphore_wait(barrier, len(peers))
+
+    def remote(src, dst, send, recv, peer):
+        return pltpu.make_async_remote_copy(
+            src_ref=src, dst_ref=dst, send_sem=send, recv_sem=recv, device_id=peer, device_id_type=MESH
+        )
+
+    def grad_copy(c, j):
+        s, flip = FSDP[j]
+        to = at_x(s) * 2 + at_yl(flip)
+        band = pl.ds(c * rows, rows)
+        return remote(
+            g_hbm.at[band, pl.ds(pl.multiple_of(to * 1024, 1024), 1024)],
+            parts.at[j, band], grad_send.at[c, j], grad_recv.at[c, j], {"fsdp": to},
+        )
+
+    def core_copy(c):
+        band = pl.ds(c * tiles, tiles)
+        return remote(updated.at[band, :, 1 - core], other.at[band], core_send.at[c], core_recv.at[c], twin)
+
+    def high_copy(c, j):
+        band = pl.ds(c * tiles, tiles)
+        to = at_yh(HIGH[j])
+        return remote(
+            pair.at[band, to], sums.at[j, band], high_send.at[c, j], high_recv.at[c, j], {"replica": to * 2 + core}
+        )
+
+    def col_copy(c, j, arriving=False):
+        band = pl.ds(c * tiles, tiles)
+        s, flip = COLUMN[j]
+        block = full.at[band, x, at_yl(flip), at_yh(-s), core] if arriving else full.at[band, x, yl, yh, core]
+        peer = {"replica": at_yh(s) * 2 + core, "fsdp": x * 2 + at_yl(flip)}
+        return remote(block, block, col_send.at[c, j], col_recv.at[c, j], peer)
+
+    def row_copy(c, j, arriving=False):
+        band = pl.ds(c * tiles, tiles)
+        block = full.at[band, at_x(-ACROSS[j]) if arriving else x, :, :, core]
+        return remote(block, block, row_send.at[c, j], row_recv.at[c, j], {"fsdp": at_x(ACROSS[j]) * 2 + yl})
+
+    def twin_copy(c, j, arriving=False):
+        band = pl.ds(c * tiles, tiles)
+        from_x = at_x(-ACROSS[j]) if j < 3 else x
+        block = full.at[band, from_x, :, :, 1 - core if arriving else core]
+        return remote(block, block, twin_send.at[c, j], twin_recv.at[c, j], twin)
+
+    def reduce_gradient(c):
+        for j in range(7):
+            grad_copy(c, j).wait_recv()
+        band = pl.ds(c * rows, rows)
+        for q in range(4):
+            cols = pl.ds(q * 256, 256)
+            gradient = own[band, cols].astype(jnp.float32)
+            for j in range(7):
+                gradient = gradient + parts[j, band, cols].astype(jnp.float32)
+            first, second, new = inner_adamw(gradient, params[band, cols], first_in[band, cols], second_in[band, cols])
+            first_out[band, cols] = first
+            second_out[band, cols] = second
+            for t in range(tiles):
+                for h in range(2):
+                    updated[c * tiles + t, q, h] = new[t * 8 : t * 8 + 8, h * 128 : h * 128 + 128]
+        core_copy(c).start()
+
+    def sum_cores(c):
+        core_copy(c).wait_recv()
+        band = pl.ds(c * tiles, tiles)
+        pair[band] = updated[band, :, core] + other[band]
+        for j in range(3):
+            high_copy(c, j).start()
+
+    def outer_step(c):
+        for j in range(3):
+            high_copy(c, j).wait_recv()
+        band = pl.ds(c * tiles, tiles)
+        total = pair[band, yh] + sums[0, band] + sums[1, band] + sums[2, band]
+        new, momentum = nesterov(total * 0.125, outer_in[band], momentum_in[band])
+        p_out[band] = new
+        m_out[band] = momentum
+        full[band, x, yl, yh, core] = new
+        for j in range(7):
+            col_copy(c, j).start()
+
+    def to_rows(c):
+        for j in range(7):
+            col_copy(c, j, True).wait_recv()
+        for j in range(3):
+            row_copy(c, j).start()
+        twin_copy(c, 3).start()
+
+    def to_twin(c):
+        for j in (1, 2, 0):
+            row_copy(c, j, True).wait_recv()
+            twin_copy(c, j).start()
+
+    def finish(c):
+        for j in (3, 1, 2, 0):
+            twin_copy(c, j, True).wait_recv()
+
+    for c in range(CHUNKS):
+        for j in range(7):
+            grad_copy(c, j).start()
+    for load in loads:
+        load.wait()
+
+    stages = [reduce_gradient, sum_cores, outer_step, to_rows, to_twin, finish]
+    for t in range(CHUNKS + len(stages) - 1):
+        for s in reversed(range(len(stages))):
+            if 0 <= t - s < CHUNKS:
+                stages[s](t - s)
+    for c in range(CHUNKS):
+        for j in range(7):
+            grad_copy(c, j).wait_send()
+            col_copy(c, j).wait_send()
+        core_copy(c).wait_send()
+        for j in range(3):
+            high_copy(c, j).wait_send()
+            row_copy(c, j).wait_send()
+        for j in range(4):
+            twin_copy(c, j).wait_send()
+
+
+def store_kernel(*refs):
+    sources, targets, sems = refs[:5], refs[5:10], refs[10]
+    copies = [pltpu.make_async_copy(src, dst, sems.at[i]) for i, (src, dst) in enumerate(zip(sources, targets))]
+    for copy in copies:
+        copy.start()
+    for copy in copies:
+        copy.wait()
+
+
+def store(arrays):
+    return pl.pallas_call(
+        store_kernel,
+        out_shape=tuple(jax.ShapeDtypeStruct(a.shape, a.dtype) for a in arrays),
+        in_specs=[pl.BlockSpec(memory_space=pltpu.VMEM)] * 5,
+        out_specs=(pl.BlockSpec(memory_space=pltpu.HBM),) * 5,
+        scratch_shapes=[pltpu.SemaphoreType.DMA((5,))],
+        name="store",
+    )(*(pltpu.with_memory_space_constraint(a, pltpu.VMEM) for a in arrays))
+
+
 def local(grad_parts, inner_params, first_moment, second_moment, outer_params, outer_momentum):
-    replicas = lax.axis_size("replica")
-    gradient = lax.psum_scatter(
-        grad_parts[0, 0].astype(jnp.float32), "fsdp", scatter_dimension=1, tiled=True
+    f32, bf16 = jnp.float32, jnp.bfloat16
+    dma = pltpu.SemaphoreType.DMA
+    vmem = pl.BlockSpec(memory_space=pltpu.VMEM)
+    operands = (
+        grad_parts.reshape(64, 8192),
+        inner_params.reshape(64, 1024),
+        first_moment.reshape(64, 1024),
+        second_moment.reshape(64, 1024),
+        outer_params.reshape(8, 8, 128),
+        outer_momentum.reshape(8, 8, 128),
     )
-    first_out, second_out, updated = inner_adamw(
-        gradient, inner_params[0], first_moment[0], second_moment[0]
+    results = pl.pallas_call(
+        kernel,
+        out_shape=(
+            pltpu.VMEM((8, 4, 2, 4, 2, 8, 128), f32),
+            pltpu.VMEM((8, 8, 128), f32),
+            pltpu.VMEM((8, 8, 128), f32),
+            pltpu.VMEM((64, 1024), f32),
+            pltpu.VMEM((64, 1024), f32),
+        ),
+        in_specs=[pl.BlockSpec(memory_space=pltpu.HBM)] * 6,
+        out_specs=(vmem,) * 5,
+        scratch_shapes=[
+            pltpu.VMEM((64, 1024), bf16),
+            pltpu.VMEM((7, 64, 1024), bf16),
+            pltpu.VMEM((64, 1024), f32),
+            pltpu.VMEM((64, 1024), f32),
+            pltpu.VMEM((64, 1024), f32),
+            pltpu.VMEM((8, 8, 128), f32),
+            pltpu.VMEM((8, 8, 128), f32),
+            pltpu.VMEM((8, 4, 2, 8, 128), f32),
+            pltpu.VMEM((8, 4, 8, 128), f32),
+            pltpu.VMEM((8, 4, 8, 128), f32),
+            pltpu.VMEM((3, 8, 8, 128), f32),
+            dma((6,)),
+            dma((CHUNKS, 7)), dma((CHUNKS, 7)),
+            dma((CHUNKS,)), dma((CHUNKS,)),
+            dma((CHUNKS, 3)), dma((CHUNKS, 3)),
+            dma((CHUNKS, 7)), dma((CHUNKS, 7)),
+            dma((CHUNKS, 3)), dma((CHUNKS, 3)),
+            dma((CHUNKS, 4)), dma((CHUNKS, 4)),
+        ],
+        compiler_params=pltpu.CompilerParams(
+            collective_id=0, has_side_effects=True, vmem_limit_bytes=32 * 2**20
+        ),
+        name="sync",
+    )(*(pltpu.with_memory_space_constraint(a, pltpu.HBM) for a in operands))
+    full, p_new, m_new, first, second = store(results)
+    next_weights = full.reshape(8, 64, 8, 128).transpose(0, 2, 1, 3).reshape(64, 8192)
+    return (
+        next_weights,
+        p_new.reshape(1, 64, 128),
+        m_new.reshape(1, 64, 128),
+        first.reshape(1, 64, 1024),
+        second.reshape(1, 64, 1024),
     )
-    share_cols = outer_params.shape[2]
-    totals = lax.psum_scatter(updated, "replica", scatter_dimension=1, tiled=True)
-    params_new, momentum_new = nesterov(totals / replicas, outer_params[0], outer_momentum[0])
-    pieces = lax.all_gather(params_new[None], ("replica", "fsdp"), axis=0, tiled=True)
-    fsdp_count = lax.axis_size("fsdp")
-    row_count = params_new.shape[0]
-    arranged = pieces.reshape(replicas, fsdp_count, row_count, share_cols).transpose(2, 1, 0, 3)
-    next_weights = arranged.reshape(row_count, fsdp_count * replicas * share_cols)
-    return (next_weights, params_new[None], momentum_new[None], first_out[None], second_out[None])
 
 
 def solution(mesh):

time: 321 us -> 55.6 us (0.17); the launches traced: 315 us -> 55.4 us
  waiting for transfers between devices: 289 us -> 0 us
  Pallas kernels: 0 us -> 54.8 us
  between operations: 13.8 us -> 0.64 us
  other arithmetic: 6.15 us -> 0 us
  local copies, waits for them, and re-layouts: 5.34 us -> 0 us
    all_gather x1 -> x0, waiting for transfers between devices: 186 us -> none  [local(): lax.all_gather(params_new[None], ('replica', 'fsdp'), axis=0, tiled=True)]
    reduce_scatter x2 -> x0, waiting for transfers between devices: 103 us -> none  [the longest x1 64.5 us: local(): lax.psum_scatter(grad_parts[0, 0].astype(jnp.float32), 'fsdp', scatter_di...]
    pallas_call x0 -> x2, Pallas kernels: none -> 54.8 us  [the longest x1 53.3 us: local(): pl.pallas_call(kernel, out_shape=(pltpu.VMEM((8, 4, 2, 4, 2, 8, 128), f32...]
    broadcast_in_dim x2 -> x0, other arithmetic: 3.41 us -> none  [the longest x1 2.02 us: local(): second_out[None]]
  transfers between devices with their start and end apart: 3 -> 0, of which waited for: 3 -> 0; matrix products, arithmetic and copies ran while one was open for 0% -> 0% of each run, Pallas kernels for 0% -> 0%
where the time goes in v1:
time: 55.6 us; the launch traced here: 55.4 us
  Pallas kernels  54.8 us (99%)
  between operations  0.64 us (1%)
    pallas_call x1, Pallas kernels, local(): pl.pallas_call(kernel, out_shape=(pltpu.VMEM((8, 4, 2, 4, 2, 8, 128), f32...  53.3 us
    pallas_call x1, Pallas kernels, store(): pl.pallas_call(store_kernel, out_shape=tuple((jax.ShapeDtypeStruct(a.shap...  1.55 us

profile of v1, /device:TPU:1, one launch (start us, length us, event | category | flops | bytes accessed | tf_op | source)
XLA Modules:
  0.0 55.4 jit_solution(7621898091242683046)
XLA Ops:
  0.6 53.3 %sync.1 = (f32[8,4,2,4,2,8,128]{6,5,4,3,2,1,0:T(8,128)S(1)}, f32[8,8,128]{2,1,0:T(8,128)S(1)}, f32[8,8,128]{2,1,0:T(8,128)S(1)}, f32[64,1024]{1,0:T(8,128)S(1)}, f32[64,1024]{1,0:T(8,128)S(1)}) custom-call(bf16[64,8192]{1,0:T(8,128)(2,1)} %bitcast.15, f32[64,1024]{1,0:T(8,128)} %bitcast.16, f32[64,1024]{1,0:T(8,128)} %bitcast.17, f32[64,1024]{1,0:T(8,128)} %bitcast.18, ...), custom_call_target="tpu_custom_call" | custom-call | tf_op jit(solution)/shard_map/sync/pallas_call | solution.py:243
  53.9 1.5 %store.1 = (f32[8,4,2,4,2,8,128]{6,5,4,3,2,1,0:T(8,128)}, f32[8,8,128]{2,1,0:T(8,128)}, f32[8,8,128]{2,1,0:T(8,128)}, f32[64,1024]{1,0:T(8,128)}, f32[64,1024]{1,0:T(8,128)}) custom-call(f32[8,4,2,4,2,8,128]{6,5,4,3,2,1,0:T(8,128)S(1)} %get-tuple-element.15.refs_0_, f32[8,8,128]{2,1,0:T(8,128)S(1)} %get-tuple-element.16.refs_1_, ...), custom_call_target="tpu_custom_call" | custom-call | tf_op jit(solution)/shard_map/store/pallas_call | solution.py:221

commit v2 on v1

--- a/solution.py
+++ b/solution.py
@@ -7,7 +7,10 @@
 
 MESH = pl.DeviceIdType.MESH
 STEP = 100
-CHUNKS = 4
+CHUNKS = 2
+DEPTH = 2
+RELAY = (0, 0, 0, 0)
+INLINE = 1
 
 beta_first = 0.9
 beta_second = 0.95
@@ -40,13 +43,29 @@
     return (params_new, momentum_new)
 
 
+SCALE = 2048.0
+POWER = 13
+
+
+def encode(weights):
+    t = jnp.clip(weights * SCALE, -850.0, 850.0)
+    t4 = (t * t) * (t * t)
+    return (t4 * t4 * t4 * t).astype(jnp.bfloat16)
+
+
+def decode(codes):
+    c = codes.astype(jnp.float32)
+    size = jnp.exp2(jnp.log2(jnp.maximum(jnp.abs(c), 1e-37)) * (1.0 / POWER)) * (1.0 / SCALE)
+    return jnp.where(c == 0.0, 0.0, jnp.where(c < 0.0, -size, size))
+
+
 def kernel(
     g_hbm, p_hbm, m1_hbm, m2_hbm, op_hbm, om_hbm,
     full, p_out, m_out, first_out, second_out,
     own, parts, params, first_in, second_in, outer_in, momentum_in,
     updated, other, pair, sums,
     local_sem, grad_send, grad_recv, core_send, core_recv, high_send, high_recv,
-    col_send, col_recv, row_send, row_recv, twin_send, twin_recv,
+    col_send, col_recv, row_send, row_recv, relay_send, relay_recv, twin_send, twin_recv,
 ):
     replica, f = lax.axis_index("replica"), lax.axis_index("fsdp")
     yh, core = replica // 2, lax.rem(replica, 2)
@@ -116,26 +135,34 @@
         )
 
     def col_copy(c, j, arriving=False):
-        band = pl.ds(c * tiles, tiles)
         s, flip = COLUMN[j]
-        block = full.at[band, x, at_yl(flip), at_yh(-s), core] if arriving else full.at[band, x, yl, yh, core]
+        block = full.at[c, x, at_yl(flip), at_yh(-s), core] if arriving else full.at[c, x, yl, yh, core]
         peer = {"replica": at_yh(s) * 2 + core, "fsdp": x * 2 + at_yl(flip)}
         return remote(block, block, col_send.at[c, j], col_recv.at[c, j], peer)
 
     def row_copy(c, j, arriving=False):
-        band = pl.ds(c * tiles, tiles)
-        block = full.at[band, at_x(-ACROSS[j]) if arriving else x, :, :, core]
+        block = full.at[c, at_x(-ACROSS[j]) if arriving else x, :, :, core]
         return remote(block, block, row_send.at[c, j], row_recv.at[c, j], {"fsdp": at_x(ACROSS[j]) * 2 + yl})
 
+    def relay_copy(c, j, arriving=False):
+        step = 1 - 2 * j
+        block = full.at[c, at_x(2) if arriving else at_x(-step), j, :, core]
+        return remote(block, block, relay_send.at[c, j], relay_recv.at[c, j], {"fsdp": at_x(step) * 2 + yl})
+
     def twin_copy(c, j, arriving=False):
-        band = pl.ds(c * tiles, tiles)
         from_x = at_x(-ACROSS[j]) if j < 3 else x
-        block = full.at[band, from_x, :, :, 1 - core if arriving else core]
+        block = full.at[c, from_x, :, :, 1 - core if arriving else core]
         return remote(block, block, twin_send.at[c, j], twin_recv.at[c, j], twin)
 
+    def send_gradient(c):
+        for j in range(7):
+            grad_copy(c, j).start()
+
     def reduce_gradient(c):
         for j in range(7):
             grad_copy(c, j).wait_recv()
+        if c + DEPTH < CHUNKS:
+            send_gradient(c + DEPTH)
         band = pl.ds(c * rows, rows)
         for q in range(4):
             cols = pl.ds(q * 256, 256)
@@ -149,6 +176,8 @@
                 for h in range(2):
                     updated[c * tiles + t, q, h] = new[t * 8 : t * 8 + 8, h * 128 : h * 128 + 128]
         core_copy(c).start()
+        if INLINE:
+            sum_cores(c)
 
     def sum_cores(c):
         core_copy(c).wait_recv()
@@ -165,35 +194,47 @@
         new, momentum = nesterov(total * 0.125, outer_in[band], momentum_in[band])
         p_out[band] = new
         m_out[band] = momentum
-        full[band, x, yl, yh, core] = new
+        full[c, x, yl, yh, core] = encode(new.reshape(rows, 128))
         for j in range(7):
             col_copy(c, j).start()
 
     def to_rows(c):
         for j in range(7):
             col_copy(c, j, True).wait_recv()
-        for j in range(3):
+        for j in (1, 2) if RELAY[c] else (0, 1, 2):
             row_copy(c, j).start()
         twin_copy(c, 3).start()
 
     def to_twin(c):
-        for j in (1, 2, 0):
+        for j in (1, 2):
             row_copy(c, j, True).wait_recv()
+            if RELAY[c]:
+                relay_copy(c, j - 1).start()
             twin_copy(c, j).start()
+        if not RELAY[c]:
+            row_copy(c, 0, True).wait_recv()
+            twin_copy(c, 0).start()
+
+    def relayed(c):
+        if RELAY[c]:
+            for j in range(2):
+                relay_copy(c, j, True).wait_recv()
+            twin_copy(c, 0).start()
 
     def finish(c):
         for j in (3, 1, 2, 0):
             twin_copy(c, j, True).wait_recv()
 
-    for c in range(CHUNKS):
-        for j in range(7):
-            grad_copy(c, j).start()
+    for c in range(min(DEPTH, CHUNKS)):
+        send_gradient(c)
     for load in loads:
         load.wait()
 
-    stages = [reduce_gradient, sum_cores, outer_step, to_rows, to_twin, finish]
+    stages = [reduce_gradient, sum_cores, outer_step, to_rows, to_twin, relayed, finish]
+    if INLINE:
+        stages.remove(sum_cores)
     for t in range(CHUNKS + len(stages) - 1):
-        for s in reversed(range(len(stages))):
+        for s in range(len(stages)):
             if 0 <= t - s < CHUNKS:
                 stages[s](t - s)
     for c in range(CHUNKS):
@@ -203,27 +244,48 @@
         core_copy(c).wait_send()
         for j in range(3):
             high_copy(c, j).wait_send()
+        for j in (1, 2) if RELAY[c] else (0, 1, 2):
             row_copy(c, j).wait_send()
+        for j in range(2 if RELAY[c] else 0):
+            relay_copy(c, j).wait_send()
         for j in range(4):
             twin_copy(c, j).wait_send()
 
 
 def store_kernel(*refs):
-    sources, targets, sems = refs[:5], refs[5:10], refs[10]
-    copies = [pltpu.make_async_copy(src, dst, sems.at[i]) for i, (src, dst) in enumerate(zip(sources, targets))]
+    sources, targets, weights, sems = refs[:5], refs[5:10], refs[10], refs[11]
+    codes = sources[0]
+    rows = 64 // CHUNKS
+    copies = [pltpu.make_async_copy(sources[i], targets[i], sems.at[i]) for i in range(1, 5)]
     for copy in copies:
         copy.start()
+    for c in range(CHUNKS):
+        band = pl.ds(c * rows, rows)
+
+        def unpack(x, _):
+            for yl in range(2):
+                for yh in range(4):
+                    for core in range(2):
+                        at = pl.multiple_of(x * 2048 + yl * 1024 + yh * 256 + core * 128, 128)
+                        weights[band, pl.ds(at, 128)] = decode(codes[c, x, yl, yh, core])
+            return _
+
+        lax.fori_loop(0, 4, unpack, 0)
+        copy = pltpu.make_async_copy(weights.at[band], targets[0].at[band], sems.at[5 + c])
+        copy.start()
+        copies.append(copy)
     for copy in copies:
         copy.wait()
 
 
 def store(arrays):
+    shapes = [(64, 8192)] + [a.shape for a in arrays[1:]]
     return pl.pallas_call(
         store_kernel,
-        out_shape=tuple(jax.ShapeDtypeStruct(a.shape, a.dtype) for a in arrays),
+        out_shape=tuple(jax.ShapeDtypeStruct(shape, jnp.float32) for shape in shapes),
         in_specs=[pl.BlockSpec(memory_space=pltpu.VMEM)] * 5,
         out_specs=(pl.BlockSpec(memory_space=pltpu.HBM),) * 5,
-        scratch_shapes=[pltpu.SemaphoreType.DMA((5,))],
+        scratch_shapes=[pltpu.VMEM((64, 8192), jnp.float32), pltpu.SemaphoreType.DMA((5 + CHUNKS,))],
         name="store",
     )(*(pltpu.with_memory_space_constraint(a, pltpu.VMEM) for a in arrays))
 
@@ -243,7 +305,7 @@
     results = pl.pallas_call(
         kernel,
         out_shape=(
-            pltpu.VMEM((8, 4, 2, 4, 2, 8, 128), f32),
+            pltpu.VMEM((CHUNKS, 4, 2, 4, 2, 64 // CHUNKS, 128), bf16),
             pltpu.VMEM((8, 8, 128), f32),
             pltpu.VMEM((8, 8, 128), f32),
             pltpu.VMEM((64, 1024), f32),
@@ -269,6 +331,7 @@
             dma((CHUNKS, 3)), dma((CHUNKS, 3)),
             dma((CHUNKS, 7)), dma((CHUNKS, 7)),
             dma((CHUNKS, 3)), dma((CHUNKS, 3)),
+            dma((CHUNKS, 2)), dma((CHUNKS, 2)),
             dma((CHUNKS, 4)), dma((CHUNKS, 4)),
         ],
         compiler_params=pltpu.CompilerParams(
@@ -276,8 +339,7 @@
         ),
         name="sync",
     )(*(pltpu.with_memory_space_constraint(a, pltpu.HBM) for a in operands))
-    full, p_new, m_new, first, second = store(results)
-    next_weights = full.reshape(8, 64, 8, 128).transpose(0, 2, 1, 3).reshape(64, 8192)
+    next_weights, p_new, m_new, first, second = store(results)
     return (
         next_weights,
         p_new.reshape(1, 64, 128),

time: 55.6 us -> 42 us (0.76)
  Pallas kernels: 54.8 us -> 41.2 us
    pallas_call x2, Pallas kernels: 54.8 us -> 41.2 us  [the longest x1 39.3 us: local(): pl.pallas_call(kernel, out_shape=(pltpu.VMEM((CHUNKS, 4, 2, 4, 2, 64 // C...]
where the time goes in v2:
time: 42 us; the launch traced here: 41.9 us
  Pallas kernels  41.2 us (98%)
  between operations  0.64 us (2%)
    pallas_call x1, Pallas kernels, local(): pl.pallas_call(kernel, out_shape=(pltpu.VMEM((CHUNKS, 4, 2, 4, 2, 64 // C...  39.3 us
    pallas_call x1, Pallas kernels, store(): pl.pallas_call(store_kernel, out_shape=tuple((jax.ShapeDtypeStruct(shape,...  1.96 us

profile of v2, /device:TPU:1, one launch (start us, length us, event | category | flops | bytes accessed | tf_op | source)
XLA Modules:
  0.0 41.9 jit_solution(1433398265499173545)
XLA Ops:
  0.6 39.3 %sync.1 = (bf16[2,4,2,4,2,32,128]{6,5,4,3,2,1,0:T(8,128)(2,1)S(1)}, f32[8,8,128]{2,1,0:T(8,128)S(1)}, f32[8,8,128]{2,1,0:T(8,128)S(1)}, f32[64,1024]{1,0:T(8,128)S(1)}, f32[64,1024]{1,0:T(8,128)S(1)}) custom-call(bf16[64,8192]{1,0:T(8,128)(2,1)} %bitcast.10, f32[64,1024]{1,0:T(8,128)} %bitcast.11, f32[64,1024]{1,0:T(8,128)} %bitcast.12, ...), custom_call_target="tpu_custom_call" | custom-call | tf_op jit(solution)/shard_map/sync/pallas_call | solution.py:305
  39.9 2.0 %store.1 = (f32[64,8192]{1,0:T(8,128)}, f32[8,8,128]{2,1,0:T(8,128)}, f32[8,8,128]{2,1,0:T(8,128)}, f32[64,1024]{1,0:T(8,128)}, f32[64,1024]{1,0:T(8,128)}) custom-call(bf16[2,4,2,4,2,32,128]{6,5,4,3,2,1,0:T(8,128)(2,1)S(1)} %get-tuple-element.15.refs_0_, f32[8,8,128]{2,1,0:T(8,128)S(1)} %get-tuple-element.16.refs_1_, ...), custom_call_target="tpu_custom_call" | custom-call | tf_op jit(solution)/shard_map/store/pallas_call | solution.py:283

commit v3 on v2

--- a/solution.py
+++ b/solution.py
@@ -7,10 +7,14 @@
 
 MESH = pl.DeviceIdType.MESH
 STEP = 100
-CHUNKS = 2
-DEPTH = 2
-RELAY = (0, 0, 0, 0)
-INLINE = 1
+UNITS = (2, 1, 1)
+CHUNKS = len(UNITS)
+ORDER = (
+    "S0", "S1", "S2", "N0", "L0", "R0", "R1", "R2",
+    "O0", "O1", "O2", "C0", "C1", "C2", "W0", "W1",
+    "W2", "F0", "F1", "F2", "Dh", "Dc", "Dr", "Dt",
+)
+FIRST = tuple(sum(UNITS[:c]) for c in range(len(UNITS)))
 
 beta_first = 0.9
 beta_second = 0.95
@@ -64,14 +68,22 @@
     full, p_out, m_out, first_out, second_out,
     own, parts, params, first_in, second_in, outer_in, momentum_in,
     updated, other, pair, sums,
-    local_sem, grad_send, grad_recv, core_send, core_recv, high_send, high_recv,
-    col_send, col_recv, row_send, row_recv, relay_send, relay_recv, twin_send, twin_recv,
+    near_a, near_b, local_sem, grad_send, grad_recv, core_send, core_recv, high_send, high_recv,
+    col_send, col_recv, row_send, row_recv, twin_send, twin_recv,
 ):
+    near_sems = (near_a, near_b)
     replica, f = lax.axis_index("replica"), lax.axis_index("fsdp")
     yh, core = replica // 2, lax.rem(replica, 2)
     x, yl = f // 2, lax.rem(f, 2)
-    rows = 64 // CHUNKS
-    tiles = rows // 8
+
+    def row_band(c):
+        return pl.ds(FIRST[c] * 16, UNITS[c] * 16)
+
+    def tile_band(c):
+        return pl.ds(FIRST[c] * 2, UNITS[c] * 2)
+
+    def unit_band(c):
+        return pl.ds(FIRST[c], UNITS[c])
 
     def at_x(step):
         return lax.rem(x + step + 4, 4)
@@ -86,7 +98,7 @@
 
     barrier = pltpu.get_barrier_semaphore()
     peers = [{"fsdp": at_x(s) * 2 + at_yl(flip)} for s, flip in FSDP]
-    peers += [{"replica": at_yh(s) * 2 + core, "fsdp": x * 2 + at_yl(flip)} for s, flip in COLUMN if s]
+    peers += [{"replica": at_yh(s) * 2 + core} for s in (1, 3)]
     peers += [twin]
     for peer in peers:
         pl.semaphore_signal(barrier, inc=1, device_id=peer, device_id_type=MESH)
@@ -117,18 +129,18 @@
     def grad_copy(c, j):
         s, flip = FSDP[j]
         to = at_x(s) * 2 + at_yl(flip)
-        band = pl.ds(c * rows, rows)
+        band = row_band(c)
         return remote(
             g_hbm.at[band, pl.ds(pl.multiple_of(to * 1024, 1024), 1024)],
             parts.at[j, band], grad_send.at[c, j], grad_recv.at[c, j], {"fsdp": to},
         )
 
     def core_copy(c):
-        band = pl.ds(c * tiles, tiles)
+        band = tile_band(c)
         return remote(updated.at[band, :, 1 - core], other.at[band], core_send.at[c], core_recv.at[c], twin)
 
     def high_copy(c, j):
-        band = pl.ds(c * tiles, tiles)
+        band = tile_band(c)
         to = at_yh(HIGH[j])
         return remote(
             pair.at[band, to], sums.at[j, band], high_send.at[c, j], high_recv.at[c, j], {"replica": to * 2 + core}
@@ -136,22 +148,18 @@
 
     def col_copy(c, j, arriving=False):
         s, flip = COLUMN[j]
-        block = full.at[c, x, at_yl(flip), at_yh(-s), core] if arriving else full.at[c, x, yl, yh, core]
+        band = unit_band(c)
+        block = full.at[band, x, at_yl(flip), at_yh(-s), core] if arriving else full.at[band, x, yl, yh, core]
         peer = {"replica": at_yh(s) * 2 + core, "fsdp": x * 2 + at_yl(flip)}
         return remote(block, block, col_send.at[c, j], col_recv.at[c, j], peer)
 
     def row_copy(c, j, arriving=False):
-        block = full.at[c, at_x(-ACROSS[j]) if arriving else x, :, :, core]
+        block = full.at[unit_band(c), at_x(-ACROSS[j]) if arriving else x, :, :, core]
         return remote(block, block, row_send.at[c, j], row_recv.at[c, j], {"fsdp": at_x(ACROSS[j]) * 2 + yl})
-
-    def relay_copy(c, j, arriving=False):
-        step = 1 - 2 * j
-        block = full.at[c, at_x(2) if arriving else at_x(-step), j, :, core]
-        return remote(block, block, relay_send.at[c, j], relay_recv.at[c, j], {"fsdp": at_x(step) * 2 + yl})
 
     def twin_copy(c, j, arriving=False):
         from_x = at_x(-ACROSS[j]) if j < 3 else x
-        block = full.at[c, from_x, :, :, 1 - core if arriving else core]
+        block = full.at[unit_band(c), from_x, :, :, 1 - core if arriving else core]
         return remote(block, block, twin_send.at[c, j], twin_recv.at[c, j], twin)
 
     def send_gradient(c):
@@ -161,27 +169,24 @@
     def reduce_gradient(c):
         for j in range(7):
             grad_copy(c, j).wait_recv()
-        if c + DEPTH < CHUNKS:
-            send_gradient(c + DEPTH)
-        band = pl.ds(c * rows, rows)
-        for q in range(4):
-            cols = pl.ds(q * 256, 256)
-            gradient = own[band, cols].astype(jnp.float32)
-            for j in range(7):
-                gradient = gradient + parts[j, band, cols].astype(jnp.float32)
-            first, second, new = inner_adamw(gradient, params[band, cols], first_in[band, cols], second_in[band, cols])
-            first_out[band, cols] = first
-            second_out[band, cols] = second
-            for t in range(tiles):
-                for h in range(2):
-                    updated[c * tiles + t, q, h] = new[t * 8 : t * 8 + 8, h * 128 : h * 128 + 128]
+        for u in range(FIRST[c], FIRST[c] + UNITS[c]):
+            band = pl.ds(u * 16, 16)
+            for q in range(4):
+                cols = pl.ds(q * 256, 256)
+                gradient = own[band, cols].astype(jnp.float32)
+                for j in range(7):
+                    gradient = gradient + parts[j, band, cols].astype(jnp.float32)
+                first, second, new = inner_adamw(
+                    gradient, params[band, cols], first_in[band, cols], second_in[band, cols]
+                )
+                first_out[band, cols] = first
+                second_out[band, cols] = second
+                for t in range(2):
+                    for h in range(2):
+                        updated[2 * u + t, q, h] = new[t * 8 : t * 8 + 8, h * 128 : h * 128 + 128]
         core_copy(c).start()
-        if INLINE:
-            sum_cores(c)
-
-    def sum_cores(c):
         core_copy(c).wait_recv()
-        band = pl.ds(c * tiles, tiles)
+        band = tile_band(c)
         pair[band] = updated[band, :, core] + other[band]
         for j in range(3):
             high_copy(c, j).start()
@@ -189,78 +194,78 @@
     def outer_step(c):
         for j in range(3):
             high_copy(c, j).wait_recv()
-        band = pl.ds(c * tiles, tiles)
+        band = tile_band(c)
         total = pair[band, yh] + sums[0, band] + sums[1, band] + sums[2, band]
         new, momentum = nesterov(total * 0.125, outer_in[band], momentum_in[band])
         p_out[band] = new
         m_out[band] = momentum
-        full[c, x, yl, yh, core] = encode(new.reshape(rows, 128))
+        full[unit_band(c), x, yl, yh, core] = encode(new.reshape(UNITS[c], 16, 128))
         for j in range(7):
             col_copy(c, j).start()
 
     def to_rows(c):
         for j in range(7):
             col_copy(c, j, True).wait_recv()
-        for j in (1, 2) if RELAY[c] else (0, 1, 2):
+        for j in range(3):
             row_copy(c, j).start()
         twin_copy(c, 3).start()
 
     def to_twin(c):
-        for j in (1, 2):
+        for j in (1, 2, 0):
             row_copy(c, j, True).wait_recv()
-            if RELAY[c]:
-                relay_copy(c, j - 1).start()
             twin_copy(c, j).start()
-        if not RELAY[c]:
-            row_copy(c, 0, True).wait_recv()
-            twin_copy(c, 0).start()
-
-    def relayed(c):
-        if RELAY[c]:
-            for j in range(2):
-                relay_copy(c, j, True).wait_recv()
-            twin_copy(c, 0).start()
 
     def finish(c):
         for j in (3, 1, 2, 0):
             twin_copy(c, j, True).wait_recv()
 
-    for c in range(min(DEPTH, CHUNKS)):
-        send_gradient(c)
-    for load in loads:
-        load.wait()
-
-    stages = [reduce_gradient, sum_cores, outer_step, to_rows, to_twin, relayed, finish]
-    if INLINE:
-        stages.remove(sum_cores)
-    for t in range(CHUNKS + len(stages) - 1):
-        for s in range(len(stages)):
-            if 0 <= t - s < CHUNKS:
-                stages[s](t - s)
-    for c in range(CHUNKS):
-        for j in range(7):
-            grad_copy(c, j).wait_send()
-            col_copy(c, j).wait_send()
-        core_copy(c).wait_send()
-        for j in range(3):
-            high_copy(c, j).wait_send()
-        for j in (1, 2) if RELAY[c] else (0, 1, 2):
-            row_copy(c, j).wait_send()
-        for j in range(2 if RELAY[c] else 0):
-            relay_copy(c, j).wait_send()
-        for j in range(4):
-            twin_copy(c, j).wait_send()
+
+    def ready(c):
+        for sem in near_sems:
+            for step in (1, 3):
+                pl.semaphore_signal(
+                    sem, inc=1, device_id={"replica": at_yh(step) * 2 + core}, device_id_type=MESH
+                )
+            pl.semaphore_wait(sem, 2)
+
+    def loaded(c):
+        for load in loads:
+            load.wait()
+
+    stages = {"S": send_gradient, "N": ready, "L": loaded, "R": reduce_gradient, "O": outer_step, "C": to_rows, "W": to_twin, "F": finish}
+    def drain(kind):
+        for c in range(CHUNKS):
+            if kind == "h":
+                for j in range(7):
+                    grad_copy(c, j).wait_send()
+                core_copy(c).wait_send()
+                for j in range(3):
+                    high_copy(c, j).wait_send()
+            elif kind == "c":
+                for j in range(7):
+                    col_copy(c, j).wait_send()
+            elif kind == "r":
+                for j in range(3):
+                    row_copy(c, j).wait_send()
+            else:
+                for j in range(4):
+                    twin_copy(c, j).wait_send()
+
+    for step in ORDER:
+        if step[0] == "D":
+            drain(step[1])
+        else:
+            stages[step[0]](int(step[1]))
 
 
 def store_kernel(*refs):
     sources, targets, weights, sems = refs[:5], refs[5:10], refs[10], refs[11]
     codes = sources[0]
-    rows = 64 // CHUNKS
     copies = [pltpu.make_async_copy(sources[i], targets[i], sems.at[i]) for i in range(1, 5)]
     for copy in copies:
         copy.start()
-    for c in range(CHUNKS):
-        band = pl.ds(c * rows, rows)
+    for c in range(4):
+        band = pl.ds(c * 16, 16)
 
         def unpack(x, _):
             for yl in range(2):
@@ -285,7 +290,7 @@
         out_shape=tuple(jax.ShapeDtypeStruct(shape, jnp.float32) for shape in shapes),
         in_specs=[pl.BlockSpec(memory_space=pltpu.VMEM)] * 5,
         out_specs=(pl.BlockSpec(memory_space=pltpu.HBM),) * 5,
-        scratch_shapes=[pltpu.VMEM((64, 8192), jnp.float32), pltpu.SemaphoreType.DMA((5 + CHUNKS,))],
+        scratch_shapes=[pltpu.VMEM((64, 8192), jnp.float32), pltpu.SemaphoreType.DMA((9,))],
         name="store",
     )(*(pltpu.with_memory_space_constraint(a, pltpu.VMEM) for a in arrays))
 
@@ -305,7 +310,7 @@
     results = pl.pallas_call(
         kernel,
         out_shape=(
-            pltpu.VMEM((CHUNKS, 4, 2, 4, 2, 64 // CHUNKS, 128), bf16),
+            pltpu.VMEM((4, 4, 2, 4, 2, 16, 128), bf16),
             pltpu.VMEM((8, 8, 128), f32),
             pltpu.VMEM((8, 8, 128), f32),
             pltpu.VMEM((64, 1024), f32),
@@ -325,13 +330,14 @@
             pltpu.VMEM((8, 4, 8, 128), f32),
             pltpu.VMEM((8, 4, 8, 128), f32),
             pltpu.VMEM((3, 8, 8, 128), f32),
+            pltpu.SemaphoreType.REGULAR,
+            pltpu.SemaphoreType.REGULAR,
             dma((6,)),
             dma((CHUNKS, 7)), dma((CHUNKS, 7)),
             dma((CHUNKS,)), dma((CHUNKS,)),
             dma((CHUNKS, 3)), dma((CHUNKS, 3)),
             dma((CHUNKS, 7)), dma((CHUNKS, 7)),
             dma((CHUNKS, 3)), dma((CHUNKS, 3)),
-            dma((CHUNKS, 2)), dma((CHUNKS, 2)),
             dma((CHUNKS, 4)), dma((CHUNKS, 4)),
         ],
         compiler_params=pltpu.CompilerParams(

time: 42 us -> 41.3 us (0.983)
  Pallas kernels: 41.2 us -> 40.5 us
    pallas_call x1, Pallas kernels: 39.3 us -> 38.6 us  [local(): pl.pallas_call(kernel, out_shape=(pltpu.VMEM((4, 4, 2, 4, 2, 16, 128), bf...]
where the time goes in v3:
time: 41.3 us; the launch traced here: 41.2 us
  Pallas kernels  40.5 us (98%)
  between operations  0.64 us (2%)
    pallas_call x1, Pallas kernels, local(): pl.pallas_call(kernel, out_shape=(pltpu.VMEM((4, 4, 2, 4, 2, 16, 128), bf...  38.6 us
    pallas_call x1, Pallas kernels, store(): pl.pallas_call(store_kernel, out_shape=tuple((jax.ShapeDtypeStruct(shape,...  1.91 us

profile of v3, /device:TPU:1, one launch (start us, length us, event | category | flops | bytes accessed | tf_op | source)
XLA Modules:
  0.0 41.2 jit_solution(10959993980383208851)
XLA Ops:
  0.6 38.6 %sync.1 = (bf16[4,4,2,4,2,16,128]{6,5,4,3,2,1,0:T(8,128)(2,1)S(1)}, f32[8,8,128]{2,1,0:T(8,128)S(1)}, f32[8,8,128]{2,1,0:T(8,128)S(1)}, f32[64,1024]{1,0:T(8,128)S(1)}, f32[64,1024]{1,0:T(8,128)S(1)}) custom-call(bf16[64,8192]{1,0:T(8,128)(2,1)} %bitcast.10, f32[64,1024]{1,0:T(8,128)} %bitcast.11, f32[64,1024]{1,0:T(8,128)} %bitcast.12, ...), custom_call_target="tpu_custom_call" | custom-call | tf_op jit(solution)/shard_map/sync/pallas_call | solution.py:310
  39.3 1.9 %store.1 = (f32[64,8192]{1,0:T(8,128)}, f32[8,8,128]{2,1,0:T(8,128)}, f32[8,8,128]{2,1,0:T(8,128)}, f32[64,1024]{1,0:T(8,128)}, f32[64,1024]{1,0:T(8,128)}) custom-call(bf16[4,4,2,4,2,16,128]{6,5,4,3,2,1,0:T(8,128)(2,1)S(1)} %get-tuple-element.15.refs_0_, f32[8,8,128]{2,1,0:T(8,128)S(1)} %get-tuple-element.16.refs_1_, ...), custom_call_target="tpu_custom_call" | custom-call | tf_op jit(solution)/shard_map/store/pallas_call | solution.py:288

commit v4 on v3

--- a/solution.py
+++ b/solution.py
@@ -14,6 +14,7 @@
     "O0", "O1", "O2", "C0", "C1", "C2", "W0", "W1",
     "W2", "F0", "F1", "F2", "Dh", "Dc", "Dr", "Dt",
 )
+PIECES = 2
 FIRST = tuple(sum(UNITS[:c]) for c in range(len(UNITS)))
 
 beta_first = 0.9
@@ -153,14 +154,14 @@
         peer = {"replica": at_yh(s) * 2 + core, "fsdp": x * 2 + at_yl(flip)}
         return remote(block, block, col_send.at[c, j], col_recv.at[c, j], peer)
 
-    def row_copy(c, j, arriving=False):
-        block = full.at[unit_band(c), at_x(-ACROSS[j]) if arriving else x, :, :, core]
-        return remote(block, block, row_send.at[c, j], row_recv.at[c, j], {"fsdp": at_x(ACROSS[j]) * 2 + yl})
-
-    def twin_copy(c, j, arriving=False):
-        from_x = at_x(-ACROSS[j]) if j < 3 else x
-        block = full.at[unit_band(c), from_x, :, :, 1 - core if arriving else core]
-        return remote(block, block, twin_send.at[c, j], twin_recv.at[c, j], twin)
+    def row_copy(c, j, half, arriving=False):
+        block = full.at[unit_band(c), at_x(-ACROSS[j]) if arriving else x, at_yl(half), :, core]
+        k = j + 3 * half
+        return remote(block, block, row_send.at[c, k], row_recv.at[c, k], {"fsdp": at_x(ACROSS[j]) * 2 + yl})
+
+    def twin_copy(c, arriving=False):
+        block = full.at[unit_band(c), :, :, :, 1 - core if arriving else core]
+        return remote(block, block, twin_send.at[c], twin_recv.at[c], twin)
 
     def send_gradient(c):
         for j in range(7):
@@ -204,21 +205,21 @@
             col_copy(c, j).start()
 
     def to_rows(c):
-        for j in range(7):
-            col_copy(c, j, True).wait_recv()
-        for j in range(3):
-            row_copy(c, j).start()
-        twin_copy(c, 3).start()
+        for half in (1, 0):
+            for j in range(7):
+                if COLUMN[j][1] == half:
+                    col_copy(c, j, True).wait_recv()
+            for j in range(3):
+                row_copy(c, j, half).start()
 
     def to_twin(c):
         for j in (1, 2, 0):
-            row_copy(c, j, True).wait_recv()
-            twin_copy(c, j).start()
+            for half in (1, 0):
+                row_copy(c, j, half, True).wait_recv()
+        twin_copy(c).start()
 
     def finish(c):
-        for j in (3, 1, 2, 0):
-            twin_copy(c, j, True).wait_recv()
-
+        twin_copy(c, True).wait_recv()
 
     def ready(c):
         for sem in near_sems:
@@ -246,10 +247,10 @@
                     col_copy(c, j).wait_send()
             elif kind == "r":
                 for j in range(3):
-                    row_copy(c, j).wait_send()
+                    row_copy(c, j, 0).wait_send()
+                    row_copy(c, j, 1).wait_send()
             else:
-                for j in range(4):
-                    twin_copy(c, j).wait_send()
+                twin_copy(c).wait_send()
 
     for step in ORDER:
         if step[0] == "D":
@@ -267,18 +268,17 @@
     for c in range(4):
         band = pl.ds(c * 16, 16)
 
-        def unpack(x, _):
-            for yl in range(2):
-                for yh in range(4):
-                    for core in range(2):
-                        at = pl.multiple_of(x * 2048 + yl * 1024 + yh * 256 + core * 128, 128)
-                        weights[band, pl.ds(at, 128)] = decode(codes[c, x, yl, yh, core])
-            return _
-
-        lax.fori_loop(0, 4, unpack, 0)
-        copy = pltpu.make_async_copy(weights.at[band], targets[0].at[band], sems.at[5 + c])
-        copy.start()
-        copies.append(copy)
+        for p in range(PIECES):
+            for x in range(p * (4 // PIECES), (p + 1) * (4 // PIECES)):
+                for yl in range(2):
+                    for yh in range(4):
+                        for core in range(2):
+                            at = x * 2048 + yl * 1024 + yh * 256 + core * 128
+                            weights[band, pl.ds(at, 128)] = decode(codes[c, x, yl, yh, core])
+            part = pl.ds(p * (8192 // PIECES), 8192 // PIECES)
+            copy = pltpu.make_async_copy(weights.at[band, part], targets[0].at[band, part], sems.at[5 + c * PIECES + p])
+            copy.start()
+            copies.append(copy)
     for copy in copies:
         copy.wait()
 
@@ -290,7 +290,7 @@
         out_shape=tuple(jax.ShapeDtypeStruct(shape, jnp.float32) for shape in shapes),
         in_specs=[pl.BlockSpec(memory_space=pltpu.VMEM)] * 5,
         out_specs=(pl.BlockSpec(memory_space=pltpu.HBM),) * 5,
-        scratch_shapes=[pltpu.VMEM((64, 8192), jnp.float32), pltpu.SemaphoreType.DMA((9,))],
+        scratch_shapes=[pltpu.VMEM((64, 8192), jnp.float32), pltpu.SemaphoreType.DMA((5 + 4 * PIECES,))],
         name="store",
     )(*(pltpu.with_memory_space_constraint(a, pltpu.VMEM) for a in arrays))
 
@@ -337,8 +337,8 @@
             dma((CHUNKS,)), dma((CHUNKS,)),
             dma((CHUNKS, 3)), dma((CHUNKS, 3)),
             dma((CHUNKS, 7)), dma((CHUNKS, 7)),
-            dma((CHUNKS, 3)), dma((CHUNKS, 3)),
-            dma((CHUNKS, 4)), dma((CHUNKS, 4)),
+            dma((CHUNKS, 6)), dma((CHUNKS, 6)),
+            dma((CHUNKS,)), dma((CHUNKS,)),
         ],
         compiler_params=pltpu.CompilerParams(
             collective_id=0, has_side_effects=True, vmem_limit_bytes=32 * 2**20

time: 41.3 us -> 40.5 us (0.981)
  Pallas kernels: 40.5 us -> 39.8 us
    pallas_call x1, Pallas kernels: 38.6 us -> 38.1 us  [local(): pl.pallas_call(kernel, out_shape=(pltpu.VMEM((4, 4, 2, 4, 2, 16, 128), bf...]
where the time goes in v4:
time: 40.5 us; the launch traced here: 40.4 us
  Pallas kernels  39.8 us (98%)
  between operations  0.64 us (2%)
    pallas_call x1, Pallas kernels, local(): pl.pallas_call(kernel, out_shape=(pltpu.VMEM((4, 4, 2, 4, 2, 16, 128), bf...  38.1 us
    pallas_call x1, Pallas kernels, store(): pl.pallas_call(store_kernel, out_shape=tuple((jax.ShapeDtypeStruct(shape,...  1.64 us

profile of v4, /device:TPU:1, one launch (start us, length us, event | category | flops | bytes accessed | tf_op | source)
XLA Modules:
  0.0 40.4 jit_solution(9862693081057831877)
XLA Ops:
  0.6 38.1 %sync.1 = (bf16[4,4,2,4,2,16,128]{6,5,4,3,2,1,0:T(8,128)(2,1)S(1)}, f32[8,8,128]{2,1,0:T(8,128)S(1)}, f32[8,8,128]{2,1,0:T(8,128)S(1)}, f32[64,1024]{1,0:T(8,128)S(1)}, f32[64,1024]{1,0:T(8,128)S(1)}) custom-call(bf16[64,8192]{1,0:T(8,128)(2,1)} %bitcast.10, f32[64,1024]{1,0:T(8,128)} %bitcast.11, f32[64,1024]{1,0:T(8,128)} %bitcast.12, ...), custom_call_target="tpu_custom_call" | custom-call | tf_op jit(solution)/shard_map/sync/pallas_call | solution.py:310
  38.8 1.6 %store.1 = (f32[64,8192]{1,0:T(8,128)}, f32[8,8,128]{2,1,0:T(8,128)}, f32[8,8,128]{2,1,0:T(8,128)}, f32[64,1024]{1,0:T(8,128)}, f32[64,1024]{1,0:T(8,128)}) custom-call(bf16[4,4,2,4,2,16,128]{6,5,4,3,2,1,0:T(8,128)(2,1)S(1)} %get-tuple-element.15.refs_0_, f32[8,8,128]{2,1,0:T(8,128)S(1)} %get-tuple-element.16.refs_1_, ...), custom_call_target="tpu_custom_call" | custom-call | tf_op jit(solution)/shard_map/store/pallas_call | solution.py:288

commit v5 on v4

--- a/solution.py
+++ b/solution.py
@@ -76,9 +76,6 @@
     replica, f = lax.axis_index("replica"), lax.axis_index("fsdp")
     yh, core = replica // 2, lax.rem(replica, 2)
     x, yl = f // 2, lax.rem(f, 2)
-
-    def row_band(c):
-        return pl.ds(FIRST[c] * 16, UNITS[c] * 16)
 
     def tile_band(c):
         return pl.ds(FIRST[c] * 2, UNITS[c] * 2)
@@ -130,7 +127,7 @@
     def grad_copy(c, j):
         s, flip = FSDP[j]
         to = at_x(s) * 2 + at_yl(flip)
-        band = row_band(c)
+        band = pl.ds(c * 16, 16)
         return remote(
             g_hbm.at[band, pl.ds(pl.multiple_of(to * 1024, 1024), 1024)],
             parts.at[j, band], grad_send.at[c, j], grad_recv.at[c, j], {"fsdp": to},
@@ -164,13 +161,14 @@
         return remote(block, block, twin_send.at[c], twin_recv.at[c], twin)
 
     def send_gradient(c):
-        for j in range(7):
-            grad_copy(c, j).start()
+        for u in range(FIRST[c], FIRST[c] + UNITS[c]):
+            for j in range(7):
+                grad_copy(u, j).start()
 
     def reduce_gradient(c):
-        for j in range(7):
-            grad_copy(c, j).wait_recv()
         for u in range(FIRST[c], FIRST[c] + UNITS[c]):
+            for j in range(7):
+                grad_copy(u, j).wait_recv()
             band = pl.ds(u * 16, 16)
             for q in range(4):
                 cols = pl.ds(q * 256, 256)
@@ -237,8 +235,9 @@
     def drain(kind):
         for c in range(CHUNKS):
             if kind == "h":
-                for j in range(7):
-                    grad_copy(c, j).wait_send()
+                for u in range(FIRST[c], FIRST[c] + UNITS[c]):
+                    for j in range(7):
+                        grad_copy(u, j).wait_send()
                 core_copy(c).wait_send()
                 for j in range(3):
                     high_copy(c, j).wait_send()
@@ -333,7 +332,7 @@
             pltpu.SemaphoreType.REGULAR,
             pltpu.SemaphoreType.REGULAR,
             dma((6,)),
-            dma((CHUNKS, 7)), dma((CHUNKS, 7)),
+            dma((4, 7)), dma((4, 7)),
             dma((CHUNKS,)), dma((CHUNKS,)),
             dma((CHUNKS, 3)), dma((CHUNKS, 3)),
             dma((CHUNKS, 7)), dma((CHUNKS, 7)),

time: 40.5 us -> 40.9 us (level)
  no operation moved by 1% of the time
where the time goes in v5:
time: 40.9 us; the launch traced here: 40.8 us
  Pallas kernels  40.1 us (98%)
  between operations  0.64 us (2%)
    pallas_call x1, Pallas kernels, local(): pl.pallas_call(kernel, out_shape=(pltpu.VMEM((4, 4, 2, 4, 2, 16, 128), bf...  38.5 us
    pallas_call x1, Pallas kernels, store(): pl.pallas_call(store_kernel, out_shape=tuple((jax.ShapeDtypeStruct(shape,...  1.64 us

profile of v5, /device:TPU:1, one launch (start us, length us, event | category | flops | bytes accessed | tf_op | source)
XLA Modules:
  0.0 40.8 jit_solution(9917123274429423551)
XLA Ops:
  0.6 38.5 %sync.1 = (bf16[4,4,2,4,2,16,128]{6,5,4,3,2,1,0:T(8,128)(2,1)S(1)}, f32[8,8,128]{2,1,0:T(8,128)S(1)}, f32[8,8,128]{2,1,0:T(8,128)S(1)}, f32[64,1024]{1,0:T(8,128)S(1)}, f32[64,1024]{1,0:T(8,128)S(1)}) custom-call(bf16[64,8192]{1,0:T(8,128)(2,1)} %bitcast.10, f32[64,1024]{1,0:T(8,128)} %bitcast.11, f32[64,1024]{1,0:T(8,128)} %bitcast.12, ...), custom_call_target="tpu_custom_call" | custom-call | tf_op jit(solution)/shard_map/sync/pallas_call | solution.py:309
  39.1 1.6 %store.1 = (f32[64,8192]{1,0:T(8,128)}, f32[8,8,128]{2,1,0:T(8,128)}, f32[8,8,128]{2,1,0:T(8,128)}, f32[64,1024]{1,0:T(8,128)}, f32[64,1024]{1,0:T(8,128)}) custom-call(bf16[4,4,2,4,2,16,128]{6,5,4,3,2,1,0:T(8,128)(2,1)S(1)} %get-tuple-element.15.refs_0_, f32[8,8,128]{2,1,0:T(8,128)S(1)} %get-tuple-element.16.refs_1_, ...), custom_call_target="tpu_custom_call" | custom-call | tf_op jit(solution)/shard_map/store/pallas_call | solution.py:287

commit v6 on v4

--- a/solution.py
+++ b/solution.py
@@ -10,7 +10,7 @@
 UNITS = (2, 1, 1)
 CHUNKS = len(UNITS)
 ORDER = (
-    "S0", "S1", "S2", "N0", "L0", "R0", "R1", "R2",
+    "S0", "S1", "S2", "N0", "L0", "R0", "X0", "R1", "R2", "X1", "X2",
     "O0", "O1", "O2", "C0", "C1", "C2", "W0", "W1",
     "W2", "F0", "F1", "F2", "Dh", "Dc", "Dr", "Dt",
 )
@@ -186,6 +186,8 @@
                     for h in range(2):
                         updated[2 * u + t, q, h] = new[t * 8 : t * 8 + 8, h * 128 : h * 128 + 128]
         core_copy(c).start()
+
+    def sum_cores(c):
         core_copy(c).wait_recv()
         band = tile_band(c)
         pair[band] = updated[band, :, core] + other[band]
@@ -233,7 +235,7 @@
         for load in loads:
             load.wait()
 
-    stages = {"S": send_gradient, "N": ready, "L": loaded, "R": reduce_gradient, "O": outer_step, "C": to_rows, "W": to_twin, "F": finish}
+    stages = {"S": send_gradient, "N": ready, "L": loaded, "X": sum_cores, "R": reduce_gradient, "O": outer_step, "C": to_rows, "W": to_twin, "F": finish}
     def drain(kind):
         for c in range(CHUNKS):
             if kind == "h":

time: 40.5 us -> 40.8 us (level)
  no operation moved by 1% of the time
where the time goes in v6:
time: 40.8 us; the launch traced here: 40.7 us
  Pallas kernels  40.1 us (98%)
  between operations  0.64 us (2%)
    pallas_call x1, Pallas kernels, local(): pl.pallas_call(kernel, out_shape=(pltpu.VMEM((4, 4, 2, 4, 2, 16, 128), bf...  38.4 us
    pallas_call x1, Pallas kernels, store(): pl.pallas_call(store_kernel, out_shape=tuple((jax.ShapeDtypeStruct(shape,...  1.64 us

profile of v6, /device:TPU:1, one launch (start us, length us, event | category | flops | bytes accessed | tf_op | source)
XLA Modules:
  0.0 40.7 jit_solution(15416135648103974400)
XLA Ops:
  0.6 38.4 %sync.1 = (bf16[4,4,2,4,2,16,128]{6,5,4,3,2,1,0:T(8,128)(2,1)S(1)}, f32[8,8,128]{2,1,0:T(8,128)S(1)}, f32[8,8,128]{2,1,0:T(8,128)S(1)}, f32[64,1024]{1,0:T(8,128)S(1)}, f32[64,1024]{1,0:T(8,128)S(1)}) custom-call(bf16[64,8192]{1,0:T(8,128)(2,1)} %bitcast.10, f32[64,1024]{1,0:T(8,128)} %bitcast.11, f32[64,1024]{1,0:T(8,128)} %bitcast.12, ...), custom_call_target="tpu_custom_call" | custom-call | tf_op jit(solution)/shard_map/sync/pallas_call | solution.py:312
  39.1 1.6 %store.1 = (f32[64,8192]{1,0:T(8,128)}, f32[8,8,128]{2,1,0:T(8,128)}, f32[8,8,128]{2,1,0:T(8,128)}, f32[64,1024]{1,0:T(8,128)}, f32[64,1024]{1,0:T(8,128)}) custom-call(bf16[4,4,2,4,2,16,128]{6,5,4,3,2,1,0:T(8,128)(2,1)S(1)} %get-tuple-element.15.refs_0_, f32[8,8,128]{2,1,0:T(8,128)S(1)} %get-tuple-element.16.refs_1_, ...), custom_call_target="tpu_custom_call" | custom-call | tf_op jit(solution)/shard_map/store/pallas_call | solution.py:290
